TPU v7x, 256 devices: a whole 4x4x8 slice. The times are simulated.
256 devices in a mesh: tgt: 64 (over x, z, core), rep: 4 (over y).
Axes of the slice: x: 4, y: 4, z: 8, core: 2. Of those that a mesh axis runs over, the one named last changes fastest.
Arguments:
- flux: bfloat16 [16384, 7808], P(('tgt', 'rep')), may hold values from 0.19921875 to 4
- ivar: bfloat16 [16384, 7808], P(('tgt', 'rep')), may hold values from 0.099609375 to 10
- row_target: int32 [16384], P(('tgt', 'rep')), may hold values from 0 to 8191, as said below
- start_w: float32 [8192, 64], P(('tgt', 'rep')), may hold values from 0.02 to 0.25
- start_h: float32 [64, 7808], P(None, 'tgt'), may hold values from 0.02 to 0.25
Outputs:
- activations: float32 [8192, 64], P(('tgt', 'rep'))
- templates: float32 [64, 7808], P(None, 'tgt')
Inputs may be any that keep to these rules, and one draw needn't show every extreme that they name: `row_target`: row i lies on device d = i // 64; its target t is owned by device t // 32, which has the same index along rep as d, i.e. (t // 32) % 4 == d % 4. The rows of one device name targets of one owning device at most 2 times, and every device reaches 2 for some owner. A target may have several rows or none.
All inputs are finite; a program needn't handle non-finite values.
Results may differ from a plain program's by a relative error of at most 0.035.
Values may be sent and summed in bfloat16 or wider, within the bound.
No kernel may reach another device: no remote copies, remote signals or barrier semaphores. Data moves between devices by JAX's collectives and lax.ppermute only.
A program may use at most 64 MiB of HBM per device.

v0:
```python
import jax
import jax.numpy as jnp
from jax import lax
from jax.sharding import PartitionSpec as P

SWEEPS = 2
PRIOR_IVAR = 0.5
EPSILON = 1e-06


def update_columns(activation, cross, gram):

    def column_step(index, current):
        gram_col = lax.dynamic_index_in_dim(gram, index, 1, keepdims=False)
        pivot = lax.dynamic_index_in_dim(gram_col, index, 0, keepdims=False)
        column = lax.dynamic_index_in_dim(current, index, 1, keepdims=False)
        wanted = lax.dynamic_index_in_dim(cross, index, 1, keepdims=False)
        fitted = jnp.dot(current, gram_col, precision=lax.Precision.HIGHEST)
        updated = jnp.maximum(column + (wanted - fitted) / (pivot + EPSILON), 0.0)
        return lax.dynamic_update_index_in_dim(current, updated, index, 1)

    return lax.fori_loop(0, activation.shape[1], column_step, activation)


def update_rows(templates, proj, gram):

    def row_step(index, current):
        gram_row = lax.dynamic_index_in_dim(gram, index, 0, keepdims=False)
        pivot = lax.dynamic_index_in_dim(gram_row, index, 0, keepdims=False)
        row_now = lax.dynamic_index_in_dim(current, index, 0, keepdims=False)
        wanted = lax.dynamic_index_in_dim(proj, index, 0, keepdims=False)
        fitted = jnp.dot(gram_row, current, precision=lax.Precision.HIGHEST)
        updated = jnp.maximum(row_now + (wanted - fitted) / (pivot + EPSILON), 0.0)
        return lax.dynamic_update_index_in_dim(current, updated, index, 0)

    return lax.fori_loop(0, templates.shape[0], row_step, templates)


def shards(flux, ivar, row_target, start_w, start_h):
    tgt_count = lax.axis_size("tgt")
    rep_count = lax.axis_size("rep")
    rows_dev = flux.shape[0]
    tgt_dev = start_w.shape[0]
    weighted = (ivar.astype(jnp.float32) * flux.astype(jnp.float32)).astype(jnp.bfloat16)
    owner_dev = row_target // tgt_dev
    peer_dev = owner_dev // rep_count
    capacity = 2 * rows_dev // tgt_count
    peer_onehot = (peer_dev[:, None] == jnp.arange(tgt_count, dtype=jnp.int32)[None, :]).astype(
        jnp.int32
    )
    running = jnp.cumsum(peer_onehot, axis=0)
    slot_index = jnp.sum(running * peer_onehot, axis=1) - 1
    place = peer_dev * capacity + slot_index
    source_row = (
        jnp.zeros((tgt_count * capacity,), jnp.int32)
        .at[place]
        .set(jnp.arange(rows_dev, dtype=jnp.int32))
    )
    filled = jnp.zeros((tgt_count * capacity,), jnp.int32).at[place].set(1)
    keep_rows = filled[:, None].astype(jnp.bfloat16)
    send_weighted = jnp.take(weighted, source_row, axis=0) * keep_rows
    send_ivar = jnp.take(ivar, source_row, axis=0) * keep_rows
    send_target = jnp.where(filled == 1, jnp.take(row_target, source_row, axis=0), -1)
    got_weighted, got_ivar, got_target = (
        lax.all_to_all(send_weighted, "tgt", split_axis=0, concat_axis=0, tiled=True),
        lax.all_to_all(send_ivar, "tgt", split_axis=0, concat_axis=0, tiled=True),
        lax.all_to_all(send_target, "tgt", split_axis=0, concat_axis=0, tiled=True),
    )
    first_target = (lax.axis_index("tgt") * rep_count + lax.axis_index("rep")) * tgt_dev
    selector = (
        got_target[None, :] - first_target == jnp.arange(tgt_dev, dtype=jnp.int32)[:, None]
    ).astype(jnp.bfloat16)
    numerator = jnp.dot(selector, got_weighted, preferred_element_type=jnp.float32)
    denominator = jnp.dot(selector, got_ivar, preferred_element_type=jnp.float32)
    coadd = (numerator / (denominator + PRIOR_IVAR)).astype(jnp.bfloat16)
    spectra = lax.all_to_all(coadd, "tgt", split_axis=1, concat_axis=0, tiled=True)
    activation = lax.all_gather(start_w, "tgt", axis=0, tiled=True)
    templates = start_h
    for sweep in range(SWEEPS):
        templ_bf = templates.astype(jnp.bfloat16)
        hgram_part = jnp.dot(templates, templates.T, precision=lax.Precision.HIGHEST)
        cross_part = jnp.dot(spectra, templ_bf.T, preferred_element_type=jnp.float32)
        cross, hgram = lax.psum((cross_part, hgram_part), "tgt")
        activation = update_columns(activation, cross, hgram)
        proj_part = lax.dot_general(
            activation.astype(jnp.bfloat16),
            spectra,
            (((0,), (0,)), ((), ())),
            preferred_element_type=jnp.float32,
        )
        wgram_part = jnp.dot(activation.T, activation, precision=lax.Precision.HIGHEST)
        proj, wgram = lax.psum((proj_part, wgram_part), "rep")
        templates = update_rows(templates, proj, wgram)
    own_w = lax.dynamic_slice_in_dim(activation, lax.axis_index("tgt") * tgt_dev, tgt_dev, 0)
    return (own_w, templates)


def solution(mesh):
    placed = (
        P(("tgt", "rep"), None),
        P(("tgt", "rep"), None),
        P(("tgt", "rep")),
        P(("tgt", "rep"), None),
        P(None, "tgt"),
    )
    return jax.shard_map(
        shards,
        mesh=mesh,
        in_specs=placed,
        out_specs=(P(("tgt", "rep"), None), P(None, "tgt")),
        check_vma=False,
    )
```

profile of v0, /device:TPU:8, one launch (start us, length us, event | category | flops | bytes accessed | tf_op | source)
XLA Modules:
  0.0 1318.5 jit_solution(9789575537605206230)
XLA Ops:
  10.4 1.6 gather_fusion
  13.6 11.9 all-to-all-start
  25.6 6.4 gather_fusion.2
  32.2 3.1 gather_fusion.1
  35.3 4.0 select_multiply_fusion.1
  39.4 1.7 all_to_all.41
  41.1 10.3 all-to-all-start.2
  51.4 5.0 all_to_all.38
  56.4 44.1 %all-to-all-done.2 = bf16[64,2,7808]{2,1,0:T(2,128)(2,1)S(1)} async-done(((bf16[64,2,7808]{2,1,0:T(2,128)(2,1)}), bf16[64,2,7808]{2,1,0:T(2,128)(2,1)S(1)}, u32[]{:S(2)}, u32[]{:S(2)}) %all-to-all-start.2) | async-done | bytes 1998880 | tf_op jit(solution)/shard_map/all_to_all | solution.py:66
  100.5 6.3 all-to-all-start.1
  107.1 4.3 all_to_all.43
  111.7 43.9 %all-to-all-done.1 = bf16[64,2,7808]{2,1,0:T(2,128)(2,1)} async-done(((bf16[64,2,7808]{2,1,0:T(2,128)(2,1)}), bf16[64,2,7808]{2,1,0:T(2,128)(2,1)}, u32[]{:S(2)}, u32[]{:S(2)}) %all-to-all-start.1) | async-done | bytes 1998880 | tf_op jit(solution)/shard_map/all_to_all | solution.py:65
  155.6 4.3 all_to_all.40
  160.3 2.1 all_to_all.44
  162.5 1.1 copy.17
  163.6 5.9 all-to-all-start.3
  169.5 17.1 %all-to-all-done.3 = bf16[32,64,122]{2,0,1:T(8,128)(2,1)S(1)} async-done(((bf16[32,64,122]{2,0,1:T(8,128)(2,1)}), bf16[32,64,122]{2,0,1:T(8,128)(2,1)S(1)}, u32[]{:S(2)}, u32[]{:S(2)}) %all-to-all-start.3) | async-done | bytes 499744 | tf_op jit(solution)/shard_map/all_to_all | solution.py:76
  186.7 1.1 fusion.28
  188.0 247.9 %psum.57 = f32[64,64]{1,0:T(8,128)S(1)} all-reduce(f32[64,64]{1,0:T(8,128)S(1)} %fusion.36), channel_id=1, replica_groups=mesh['tgt'=64,'rep'=4] {'tgt'}, use_global_device_ids=true, to_apply=%region_0.1 | all-reduce | flops 4096 | bytes 32768 | tf_op jit(solution)/shard_map/psum | solution.py:83
  436.0 47.2 %all_gather.3 = f32[2048,64]{1,0:T(8,128)S(1)} all-gather(f32[32,64]{1,0:T(8,128)S(1)} %copy-done.4), channel_id=1, replica_groups=mesh['tgt'=64,'rep'=4] {'tgt'}, dimensions={0}, use_global_device_ids=true | all-gather | bytes 532480 | tf_op jit(solution)/shard_map/all_gather | solution.py:77
  483.5 181.6 %while.64 = (s32[]{:T(128)}, f32[2048,64]{0,1:T(8,128)S(1)}, f32[2048,64]{0,1:T(8,128)}, f32[64,64]{0,1:T(8,128)S(1)}, s32[]{:T(128)}, /*index=5*/s32[]{:T(128)}, s32[]{:T(128)}, f32[1,1]{0,1:T(1,128)}) while((s32[]{:T(128)}, f32[2048,64]{0,1:T(8,128)S(1)}, f32[2048,64]{0,1:T(8,128)}, f32[64,64]{0,1:T(8,128)S(1)}, s32[]{:T(128)}, ...), condition=%wide.region_7.9_spmd, body=%wide.region_6.8_spmd.sunk | while | flops 1581060 | bytes 615053 | solution.py:22
  483.5 0.9 constant_dynamic-slice_fusion.20
  486.4 0.9 constant_dynamic-slice_fusion.20
  497.7 0.9 constant_dynamic-slice_fusion.20
  500.6 0.9 constant_dynamic-slice_fusion.20
  665.9 14.8 %all-reduce.1 = (f32[64,122]{1,0:T(8,128)S(1)}, f32[64,64]{1,0:T(8,128)S(1)}) all-reduce(f32[64,122]{1,0:T(8,128)S(1)} %fusion.23, f32[64,64]{1,0:T(8,128)S(1)} %fusion.37), channel_id=1, replica_groups=mesh['tgt'=64,'rep'=4] {'rep'}, use_global_device_ids=true, to_apply=%region_9.11 | all-reduce | flops 11904 | bytes 95232 | tf_op jit(solution)/shard_map/psum | solution.py:92
  680.7 91.4 %while.65 = (s32[]{:T(128)}, f32[64,122]{1,0:T(8,128)S(1)}, f32[64,122]{1,0:T(8,128)S(1)}, f32[64,64]{1,0:T(8,128)S(1)}, s32[]{:T(128)}, /*index=5*/s32[]{:T(128)}, s32[]{:T(128)}, f32[1,1]{1,0:T(1,128)}) while((s32[]{:T(128)}, f32[64,122]{1,0:T(8,128)S(1)}, f32[64,122]{1,0:T(8,128)S(1)}, f32[64,64]{1,0:T(8,128)S(1)}, s32[]{:T(128)}, ...), condition=%wide.region_11.13_spmd, body=%wide.region_10.12_spmd.sunk | while | flops 94188 | bytes 37433 | solution.py:36
  772.2 1.1 fusion.26
  773.5 246.2 %psum.61 = f32[64,64]{1,0:T(8,128)S(1)} all-reduce(f32[64,64]{1,0:T(8,128)S(1)} %fusion.38), channel_id=1, replica_groups=mesh['tgt'=64,'rep'=4] {'tgt'}, use_global_device_ids=true, to_apply=%region_12.14 | all-reduce | flops 4096 | bytes 32768 | tf_op jit(solution)/shard_map/psum | solution.py:83
  1019.7 181.6 %while.66 = (s32[]{:T(128)}, f32[2048,64]{0,1:T(8,128)S(1)}, f32[2048,64]{0,1:T(8,128)}, f32[64,64]{0,1:T(8,128)S(1)}, s32[]{:T(128)}, /*index=5*/s32[]{:T(128)}, s32[]{:T(128)}, f32[1,1]{0,1:T(1,128)}) while((s32[]{:T(128)}, f32[2048,64]{0,1:T(8,128)S(1)}, f32[2048,64]{0,1:T(8,128)}, f32[64,64]{0,1:T(8,128)S(1)}, s32[]{:T(128)}, ...), condition=%wide.region_15.17_spmd, body=%wide.region_14.16_spmd.sunk | while | flops 1581060 | bytes 615053 | solution.py:22
  1202.4 17.2 %all-reduce = (f32[64,122]{1,0:T(8,128)S(1)}, f32[64,64]{1,0:T(8,128)S(1)}) all-reduce(f32[64,122]{1,0:T(8,128)S(1)} %fusion.21, f32[64,64]{1,0:T(8,128)S(1)} %fusion.39), channel_id=1, replica_groups=mesh['tgt'=64,'rep'=4] {'rep'}, use_global_device_ids=true, to_apply=%region_17.19 | all-reduce | flops 11904 | bytes 95232 | tf_op jit(solution)/shard_map/psum | solution.py:92
  1219.7 91.4 %while.67 = (s32[]{:T(128)}, f32[64,122]{1,0:T(8,128)S(1)}, f32[64,122]{1,0:T(8,128)S(1)}, f32[64,64]{1,0:T(8,128)S(1)}, s32[]{:T(128)}, /*index=5*/s32[]{:T(128)}, s32[]{:T(128)}, f32[1,1]{1,0:T(1,128)}) while((s32[]{:T(128)}, f32[64,122]{1,0:T(8,128)S(1)}, f32[64,122]{1,0:T(8,128)S(1)}, f32[64,64]{1,0:T(8,128)S(1)}, s32[]{:T(128)}, ...), condition=%wide.region_19.21_spmd, body=%wide.region_18.20_spmd.sunk | while | flops 94188 | bytes 37433 | solution.py:36
  (1067 shorter events, 372.9 us)
Async XLA Ops:
  13.6 27.5 %all-to-all-start = ((s32[64,2,1]{1,2,0:T(1,128)}), s32[64,2,1]{1,2,0:T(1,128)S(1)}, u32[]{:S(2)}, u32[]{:S(2)}) async-start(s32[64,2,1]{1,2,0:T(1,128)} %bitcast.26), calls=%async_computation | async-start | bytes 65536 | tf_op jit(solution)/shard_map/all_to_all | solution.py:67
  25.5 6.4 copy-start
  25.5 6.4 copy-start.3
  41.1 59.4 %all-to-all-start.2 = ((bf16[64,2,7808]{2,1,0:T(2,128)(2,1)}), bf16[64,2,7808]{2,1,0:T(2,128)(2,1)S(1)}, u32[]{:S(2)}, u32[]{:S(2)}) async-start(bf16[64,2,7808]{2,1,0:T(2,128)(2,1)} %all_to_all.41), calls=%async_computation.2 | async-start | bytes 3997696 | tf_op jit(solution)/shard_map/all_to_all | solution.py:66
  100.5 6.3 copy-start.2
  100.5 55.1 %all-to-all-start.1 = ((bf16[64,2,7808]{2,1,0:T(2,128)(2,1)}), bf16[64,2,7808]{2,1,0:T(2,128)(2,1)}, u32[]{:S(2)}, u32[]{:S(2)}) async-start(bf16[64,2,7808]{2,1,0:T(2,128)(2,1)} %all_to_all.38), calls=%async_computation.1 | async-start | bytes 3997696 | tf_op jit(solution)/shard_map/all_to_all | solution.py:65
  162.4 273.6 %copy-start.4 = (f32[32,64]{1,0:T(8,128)S(1)}, f32[32,64]{1,0:T(8,128)}, u32[]{:S(2)}) copy-start(f32[32,64]{1,0:T(8,128)} %param.18) | copy-start | bytes 24580
  163.6 23.1 %all-to-all-start.3 = ((bf16[32,64,122]{2,0,1:T(8,128)(2,1)}), bf16[32,64,122]{2,0,1:T(8,128)(2,1)S(1)}, u32[]{:S(2)}, u32[]{:S(2)}) async-start(bf16[32,64,122]{2,0,1:T(8,128)(2,1)} %copy.17), calls=%async_computation.3 | async-start | bytes 1048576 | tf_op jit(solution)/shard_map/all_to_all | solution.py:76
  169.5 314.1 %all-reduce.5.cloned.1.call-start = ((), (), s32[]{:S(2)}) async-start(), calls=%async_computation.4 | async-start | bytes 1048576 | tf_op jit(solution)/shard_map/psum | solution.py:83
  187.8 831.9 %all-reduce.7.cloned.1.call-start = ((), (), s32[]{:S(2)}) async-start(), calls=%async_computation.5 | async-start | bytes 1048576 | tf_op jit(solution)/shard_map/psum | solution.py:83
  1311.1 0.6 copy-start.1
Sparse Core Ops, SparseCore 0:
  187.9 178.6 all-reduce.4
  773.4 179.9 all-reduce.6
where the time goes:
time: 1330 us; the launch traced here: 1320 us
  blocking collectives  573 us (43%)
  local copies, waits for them, and re-layouts  335 us (25%)
  loops' own time  179 us (13%)
  waiting for transfers between devices  105 us (8%)
  matrix products  70.2 us (5%)
  starting transfers between devices  34.5 us (3%)
  between operations  14.4 us (1%)
    psum x2, blocking collectives, shards(): cross, hgram = lax.psum((cross_part, hgram_part), 'tgt')  494 us
    dynamic_slice x128, local copies, waits for them, and re-layouts, column_step(): wanted = lax.dynamic_index_in_dim(cross, index, 1, keepdims=False)  110 us
    another operation x2, loops' own time, update_columns(): return lax.fori_loop(0, activation.shape[1], column_step, activation)  93.4 us
    dynamic_slice x128, local copies, waits for them, and re-layouts, column_step(): pivot = lax.dynamic_index_in_dim(gram_col, index, 0, keepdims=False)  85.8 us
    another operation x2, loops' own time, update_rows(): return lax.fori_loop(0, templates.shape[0], row_step, templates)  85.8 us
    dynamic_slice x128, local copies, waits for them, and re-layouts, row_step(): pivot = lax.dynamic_index_in_dim(gram_row, index, 0, keepdims=False)  75.3 us
    all_gather x1, blocking collectives, shards(): activation = lax.all_gather(start_w, 'tgt', axis=0, tiled=True)  47.2 us
    dot_general x128, matrix products, column_step(): fitted = jnp.dot(current, gram_col, precision=lax.Precision.HIGHEST)  46.8 us
  transfers between devices with their start and end apart: 6, of which 3 were waited for; matrix products, arithmetic and copies ran while one was open for 1% of the time, Pallas kernels for 0%

commit v1 on v0

--- a/solution.py
+++ b/solution.py
@@ -74,7 +74,9 @@
     denominator = jnp.dot(selector, got_ivar, preferred_element_type=jnp.float32)
     coadd = (numerator / (denominator + PRIOR_IVAR)).astype(jnp.bfloat16)
     spectra = lax.all_to_all(coadd, "tgt", split_axis=1, concat_axis=0, tiled=True)
-    activation = lax.all_gather(start_w, "tgt", axis=0, tiled=True)
+    activation = jnp.concatenate(
+        lax.all_to_all(jnp.stack([start_w] * lax.axis_size("tgt")), "tgt", 0, 0), axis=0
+    )
     templates = start_h
     for sweep in range(SWEEPS):
         templ_bf = templates.astype(jnp.bfloat16)

time: 1330 us -> 1290 us (0.970)
  blocking collectives: 573 us -> 530 us
    all_gather x1 -> x0, blocking collectives: 47.2 us -> none  [shards(): activation = lax.all_gather(start_w, 'tgt', axis=0, tiled=True)]
  transfers between devices with their start and end apart: 6 -> 7, of which waited for: 3 -> 3; matrix products, arithmetic and copies ran while one was open for 1% -> 2% of each run, Pallas kernels for 0% -> 0%
where the time goes in v1:
time: 1290 us; the launch traced here: 1280 us
  blocking collectives  530 us (41%)
  local copies, waits for them, and re-layouts  333 us (26%)
  loops' own time  176 us (14%)
  waiting for transfers between devices  104 us (8%)
  matrix products  71 us (6%)
  starting transfers between devices  40.9 us (3%)
  between operations  14.4 us (1%)
    psum x2, blocking collectives, shards(): cross, hgram = lax.psum((cross_part, hgram_part), 'tgt')  498 us
    dynamic_slice x128, local copies, waits for them, and re-layouts, column_step(): wanted = lax.dynamic_index_in_dim(cross, index, 1, keepdims=False)  110 us
    another operation x2, loops' own time, update_columns(): return lax.fori_loop(0, activation.shape[1], column_step, activation)  90.5 us
    another operation x2, loops' own time, update_rows(): return lax.fori_loop(0, templates.shape[0], row_step, templates)  85.8 us
    dynamic_slice x128, local copies, waits for them, and re-layouts, column_step(): pivot = lax.dynamic_index_in_dim(gram_col, index, 0, keepdims=False)  80.6 us
    dynamic_slice x128, local copies, waits for them, and re-layouts, row_step(): pivot = lax.dynamic_index_in_dim(gram_row, index, 0, keepdims=False)  75.3 us
    dot_general x128, matrix products, column_step(): fitted = jnp.dot(current, gram_col, precision=lax.Precision.HIGHEST)  46.8 us
    all_to_all x1, waiting for transfers between devices, shards(): lax.all_to_all(send_ivar, 'tgt', split_axis=0, concat_axis=0, tiled=True)  44.1 us
  transfers between devices with their start and end apart: 7, of which 3 were waited for; matrix products, arithmetic and copies ran while one was open for 2% of the time, Pallas kernels for 0%

profile of v1, /device:TPU:8, one launch (start us, length us, event | category | flops | bytes accessed | tf_op | source)
XLA Modules:
  0.0 1278.3 jit_solution(6263167141733972987)
XLA Ops:
  10.4 1.6 gather_fusion
  13.6 11.9 all-to-all-start.1
  25.6 6.4 gather_fusion.2
  32.2 3.1 gather_fusion.1
  35.3 4.0 select_multiply_fusion.1
  39.4 1.7 all_to_all.45
  41.1 10.3 all-to-all-start.3
  51.4 5.0 all_to_all.42
  56.4 44.1 %all-to-all-done.3 = bf16[64,2,7808]{2,1,0:T(2,128)(2,1)S(1)} async-done(((bf16[64,2,7808]{2,1,0:T(2,128)(2,1)}), bf16[64,2,7808]{2,1,0:T(2,128)(2,1)S(1)}, u32[]{:S(2)}, u32[]{:S(2)}) %all-to-all-start.3) | async-done | bytes 1998880 | tf_op jit(solution)/shard_map/all_to_all | solution.py:66
  100.5 6.3 all-to-all-start.2
  107.1 4.3 all_to_all.47
  111.7 43.9 %all-to-all-done.2 = bf16[64,2,7808]{2,1,0:T(2,128)(2,1)} async-done(((bf16[64,2,7808]{2,1,0:T(2,128)(2,1)}), bf16[64,2,7808]{2,1,0:T(2,128)(2,1)}, u32[]{:S(2)}, u32[]{:S(2)}) %all-to-all-start.2) | async-done | bytes 1998880 | tf_op jit(solution)/shard_map/all_to_all | solution.py:65
  155.6 4.3 all_to_all.44
  159.9 1.2 fusion.20
  161.1 3.2 all_to_all.48
  164.3 1.2 copy.22
  165.4 5.9 all-to-all-start.4
  171.4 1.4 reshape.124
  172.9 15.6 %all-to-all-done.4 = bf16[32,64,122]{2,0,1:T(8,128)(2,1)S(1)} async-done(((bf16[32,64,122]{2,0,1:T(8,128)(2,1)}), bf16[32,64,122]{2,0,1:T(8,128)(2,1)S(1)}, u32[]{:S(2)}, u32[]{:S(2)}) %all-to-all-start.4) | async-done | bytes 499744 | tf_op jit(solution)/shard_map/all_to_all | solution.py:76
  188.5 6.4 all-to-all-start
  195.0 1.1 fusion.28
  196.4 251.8 %psum.57 = f32[64,64]{1,0:T(8,128)S(1)} all-reduce(f32[64,64]{1,0:T(8,128)S(1)} %fusion.36), channel_id=1, replica_groups=mesh['tgt'=64,'rep'=4] {'tgt'}, use_global_device_ids=true, to_apply=%region_0.1 | all-reduce | flops 4096 | bytes 32768 | tf_op jit(solution)/shard_map/psum | solution.py:85
  448.8 1.9 reduce.4
  451.5 173.5 %while.64 = (s32[]{:T(128)}, f32[2048,64]{0,1:T(8,128)S(1)}, f32[2048,64]{0,1:T(8,128)}, f32[64,64]{0,1:T(8,128)S(1)}, s32[]{:T(128)}, /*index=5*/s32[]{:T(128)}, s32[]{:T(128)}, f32[1,1]{0,1:T(1,128)}) while((s32[]{:T(128)}, f32[2048,64]{0,1:T(8,128)S(1)}, f32[2048,64]{0,1:T(8,128)}, f32[64,64]{0,1:T(8,128)S(1)}, s32[]{:T(128)}, ...), condition=%wide.region_7.9_spmd, body=%wide.region_6.8_spmd.sunk | while | flops 1581060 | bytes 615053 | solution.py:22
  454.2 0.9 constant_dynamic-slice_fusion.20
  625.7 14.8 %all-reduce.1 = (f32[64,122]{1,0:T(8,128)S(1)}, f32[64,64]{1,0:T(8,128)S(1)}) all-reduce(f32[64,122]{1,0:T(8,128)S(1)} %fusion.23, f32[64,64]{1,0:T(8,128)S(1)} %fusion.37), channel_id=1, replica_groups=mesh['tgt'=64,'rep'=4] {'rep'}, use_global_device_ids=true, to_apply=%region_9.11 | all-reduce | flops 11904 | bytes 95232 | tf_op jit(solution)/shard_map/psum | solution.py:94
  640.6 91.4 %while.65 = (s32[]{:T(128)}, f32[64,122]{1,0:T(8,128)S(1)}, f32[64,122]{1,0:T(8,128)S(1)}, f32[64,64]{1,0:T(8,128)S(1)}, s32[]{:T(128)}, /*index=5*/s32[]{:T(128)}, s32[]{:T(128)}, f32[1,1]{1,0:T(1,128)}) while((s32[]{:T(128)}, f32[64,122]{1,0:T(8,128)S(1)}, f32[64,122]{1,0:T(8,128)S(1)}, f32[64,64]{1,0:T(8,128)S(1)}, s32[]{:T(128)}, ...), condition=%wide.region_11.13_spmd, body=%wide.region_10.12_spmd.sunk | while | flops 94188 | bytes 37433 | solution.py:36
  732.0 1.1 fusion.26
  733.3 246.3 %psum.61 = f32[64,64]{1,0:T(8,128)S(1)} all-reduce(f32[64,64]{1,0:T(8,128)S(1)} %fusion.38), channel_id=1, replica_groups=mesh['tgt'=64,'rep'=4] {'tgt'}, use_global_device_ids=true, to_apply=%region_12.14 | all-reduce | flops 4096 | bytes 32768 | tf_op jit(solution)/shard_map/psum | solution.py:85
  979.7 181.6 %while.66 = (s32[]{:T(128)}, f32[2048,64]{0,1:T(8,128)S(1)}, f32[2048,64]{0,1:T(8,128)}, f32[64,64]{0,1:T(8,128)S(1)}, s32[]{:T(128)}, /*index=5*/s32[]{:T(128)}, s32[]{:T(128)}, f32[1,1]{0,1:T(1,128)}) while((s32[]{:T(128)}, f32[2048,64]{0,1:T(8,128)S(1)}, f32[2048,64]{0,1:T(8,128)}, f32[64,64]{0,1:T(8,128)S(1)}, s32[]{:T(128)}, ...), condition=%wide.region_15.17_spmd, body=%wide.region_14.16_spmd.sunk | while | flops 1581060 | bytes 615053 | solution.py:22
  1162.4 17.1 %all-reduce = (f32[64,122]{1,0:T(8,128)S(1)}, f32[64,64]{1,0:T(8,128)S(1)}) all-reduce(f32[64,122]{1,0:T(8,128)S(1)} %fusion.21, f32[64,64]{1,0:T(8,128)S(1)} %fusion.39), channel_id=1, replica_groups=mesh['tgt'=64,'rep'=4] {'rep'}, use_global_device_ids=true, to_apply=%region_17.19 | all-reduce | flops 11904 | bytes 95232 | tf_op jit(solution)/shard_map/psum | solution.py:94
  1179.5 91.4 %while.67 = (s32[]{:T(128)}, f32[64,122]{1,0:T(8,128)S(1)}, f32[64,122]{1,0:T(8,128)S(1)}, f32[64,64]{1,0:T(8,128)S(1)}, s32[]{:T(128)}, /*index=5*/s32[]{:T(128)}, s32[]{:T(128)}, f32[1,1]{1,0:T(1,128)}) while((s32[]{:T(128)}, f32[64,122]{1,0:T(8,128)S(1)}, f32[64,122]{1,0:T(8,128)S(1)}, f32[64,64]{1,0:T(8,128)S(1)}, s32[]{:T(128)}, ...), condition=%wide.region_19.21_spmd, body=%wide.region_18.20_spmd.sunk | while | flops 94188 | bytes 37433 | solution.py:36
  (1073 shorter events, 370.9 us)
Async XLA Ops:
  13.6 27.5 %all-to-all-start.1 = ((s32[64,2,1]{1,2,0:T(1,128)}), s32[64,2,1]{1,2,0:T(1,128)S(1)}, u32[]{:S(2)}, u32[]{:S(2)}) async-start(s32[64,2,1]{1,2,0:T(1,128)} %bitcast.27), calls=%async_computation.1 | async-start | bytes 65536 | tf_op jit(solution)/shard_map/all_to_all | solution.py:67
  25.5 6.4 copy-start
  25.5 6.4 copy-start.3
  41.1 59.4 %all-to-all-start.3 = ((bf16[64,2,7808]{2,1,0:T(2,128)(2,1)}), bf16[64,2,7808]{2,1,0:T(2,128)(2,1)S(1)}, u32[]{:S(2)}, u32[]{:S(2)}) async-start(bf16[64,2,7808]{2,1,0:T(2,128)(2,1)} %all_to_all.45), calls=%async_computation.3 | async-start | bytes 3997696 | tf_op jit(solution)/shard_map/all_to_all | solution.py:66
  100.5 6.3 copy-start.2
  100.5 55.1 %all-to-all-start.2 = ((bf16[64,2,7808]{2,1,0:T(2,128)(2,1)}), bf16[64,2,7808]{2,1,0:T(2,128)(2,1)}, u32[]{:S(2)}, u32[]{:S(2)}) async-start(bf16[64,2,7808]{2,1,0:T(2,128)(2,1)} %all_to_all.42), calls=%async_computation.2 | async-start | bytes 3997696 | tf_op jit(solution)/shard_map/all_to_all | solution.py:65
  161.1 10.2 copy-start.4
  165.4 23.1 %all-to-all-start.4 = ((bf16[32,64,122]{2,0,1:T(8,128)(2,1)}), bf16[32,64,122]{2,0,1:T(8,128)(2,1)S(1)}, u32[]{:S(2)}, u32[]{:S(2)}) async-start(bf16[32,64,122]{2,0,1:T(8,128)(2,1)} %copy.22), calls=%async_computation.4 | async-start | bytes 1048576 | tf_op jit(solution)/shard_map/all_to_all | solution.py:76
  188.5 259.8 %all-to-all-start = ((f32[64,1,2048]{2,1,0:T(1,128)}), f32[64,1,2048]{2,1,0:T(1,128)S(1)}, u32[]{:S(2)}, u32[]{:S(2)}) async-start(f32[64,1,2048]{2,1,0:T(1,128)} %reshape.124), calls=%async_computation | async-start | bytes 1048576 | tf_op jit(solution)/shard_map/all_to_all | solution.py:78
  194.9 256.5 %all-reduce.5.cloned.1.call-start = ((), (), s32[]{:S(2)}) async-start(), calls=%async_computation.5 | async-start | bytes 1048576 | tf_op jit(solution)/shard_map/psum | solution.py:85
  196.1 783.5 %all-reduce.7.cloned.1.call-start = ((), (), s32[]{:S(2)}) async-start(), calls=%async_computation.6 | async-start | bytes 1048576 | tf_op jit(solution)/shard_map/psum | solution.py:85
  1270.9 0.6 copy-start.1
Sparse Core Ops, SparseCore 0:
  199.2 182.7 all-reduce.4
  733.2 176.5 all-reduce.6
